TPU v7x, 32 devices: a whole 2x2x4 slice. The times are simulated.
32 devices in a mesh: ctx: 4 (over y, x), tile: 8 (over z, core).
Axes of the slice: x: 2, y: 2, z: 4, core: 2. Of those that a mesh axis runs over, the one named last changes fastest.
Arguments:
- syndrome_bits: int32 [8, 2, 32, 256], P(None, None, 'ctx', 'tile'), may hold values from 0 to 1
- region_assign: int32 [16, 128], P('ctx', 'tile'), may hold values from 0 to 127
- state_in: bfloat16 [32, 256, 512], P('ctx', 'tile'), may hold values from -3 to 3
- bit_to_candidate: float32 [2, 512], replicated, may hold values from -5 to 5
- bit_to_gate: float32 [2, 512], replicated, may hold values from -5 to 5
- conv_weight: bfloat16 [9, 512, 512], replicated, may hold values from -0.09375 to 0.09375
- gate_weight: bfloat16 [512, 512], replicated, may hold values from -0.25 to 0.25
- gate_bias: float32 [512], replicated, may hold values from -4 to 1
- pool_weight: bfloat16 [512, 1024], replicated, may hold values from -0.25 to 0.25
- region_embed: bfloat16 [512, 1024], P('ctx'), may hold values from -6 to 6
- attn_norm_gain: float32 [1024], replicated, may hold values from 0.1 to 1.9
- query_weight: bfloat16 [1024, 1024], replicated
- key_weight: bfloat16 [1024, 1024], replicated
- value_weight: bfloat16 [1024, 1024], replicated, may hold values from -0.1875 to 0.1875
- out_weight: bfloat16 [1024, 1024], replicated, may hold values from -0.1875 to 0.1875
- mlp_norm_gain: float32 [1024], replicated, may hold values from 0.1 to 1.9
- mlp_up: bfloat16 [1024, 2048], replicated, may hold values from -0.1875 to 0.1875
- mlp_down: bfloat16 [2048, 1024], replicated, may hold values from -0.125 to 0.125
- return_weight: bfloat16 [1024, 512], replicated, may hold values from -0.1875 to 0.1875
Outputs:
- state_out: bfloat16 [32, 256, 512], P('ctx', 'tile')
- context_out: bfloat16 [512, 1024], P('ctx')
All inputs are finite; a program needn't handle non-finite values.
Results may differ from a plain program's by a relative error of at most 0.02.
Values may be sent and summed in bfloat16 or wider, within the bound.
No kernel may reach another device: no remote copies, remote signals or barrier semaphores. Data moves between devices by JAX's collectives and lax.ppermute only.
A program may use at most 128 MiB of HBM per device.

v0:
```python
import functools
import math

import jax
import jax.numpy as jnp
from jax import lax
from jax.experimental import pallas as pl
from jax.experimental.pallas import tpu as pltpu
from jax.sharding import PartitionSpec as P

HEADS = 8
HDIM = 128
ROUNDS = 8
HALF = ROUNDS // 2
LANES = 128
F32 = jnp.float32
BF16 = jnp.bfloat16
MIB = 2**20

REGION_LANE, LOW_LANE, ONE_LANE = 2 * ROUNDS, 32, 64


def shifted(value, down, right):
    bands, tiles = lax.axis_size("ctx"), lax.axis_size("tile")
    pairs = [
        (i * tiles + j, (i + down) * tiles + j + right)
        for i in range(bands)
        for j in range(tiles)
        if 0 <= i + down < bands and 0 <= j + right < tiles
    ]
    return lax.ppermute(value, ("ctx", "tile"), pairs)


def exchange(sides):
    top, bottom, first, last, top_first, top_last, bottom_first, bottom_last = sides
    return (
        shifted(bottom, 1, 0),
        shifted(top, -1, 0),
        shifted(last, 0, 1),
        shifted(first, 0, -1),
        shifted(bottom_last, 1, 1),
        shifted(bottom_first, 1, -1),
        shifted(top_last, -1, 1),
        shifted(top_first, -1, -1),
    )


def matmul(left, right):
    return jnp.dot(left, right, preferred_element_type=F32)


def matmul_nt(left, right):
    return lax.dot_general(left, right, (((1,), (1,)), ((), ())), preferred_element_type=F32)


def two_parts(values):
    high = values.astype(BF16)
    return high, (values - high.astype(F32)).astype(BF16)


def select(member, values):
    high, low = two_parts(values)
    return matmul(member, high) + matmul(member, low)


def rms_norm(values, gain):
    return values * lax.rsqrt(jnp.mean(values * values, axis=-1, keepdims=True) + 1e-05) * gain


def iota(shape, dim):
    return lax.broadcasted_iota(jnp.int32, shape, dim)


def one_hot(condition):
    return jnp.where(condition, 1.0, 0.0).astype(BF16)


def call(kernel, name, operands, outs, scratch=(), in_hbm=(), scalars=(), grant=60, flops=0, moved=MIB):
    def spec(index):
        if index in in_hbm:
            return pl.BlockSpec(memory_space=pltpu.HBM)
        return pl.BlockSpec(memory_space=pltpu.SMEM if index in scalars else pltpu.VMEM)

    return pl.pallas_call(
        kernel,
        out_shape=outs,
        in_specs=[spec(index) for index in range(len(operands))],
        out_specs=[pl.BlockSpec(memory_space=pltpu.VMEM)] * len(outs),
        scratch_shapes=scratch,
        compiler_params=pltpu.CompilerParams(vmem_limit_bytes=grant * MIB),
        cost_estimate=pl.CostEstimate(flops=flops, bytes_accessed=moved, transcendentals=0),
        name=name,
    )(*operands)


def array(count, lanes, dtype):
    return jax.ShapeDtypeStruct((count, lanes), dtype)


def side_arrays(half, lanes):
    edge = HALF * HALF
    return [array(count, lanes, BF16) for count in (half, half, 2 * edge, 2 * edge, edge, edge, edge, edge)]


def write_sides(sides, rows, cols):
    top, bottom, first, last, *corners = sides
    edges = []
    for r, values in enumerate(rows):
        half = (top, bottom)[r // HALF]
        half[r % HALF * cols : (r % HALF + 1) * cols] = values.astype(BF16)
    for begin in (0, cols - HALF):
        edges.append(jnp.concatenate([values[begin : begin + HALF] for values in rows]).astype(BF16))
    first[...], last[...] = edges
    edge = HALF * HALF
    for at, corner in enumerate(corners):
        corner[...] = edges[at % 2][at // 2 * edge : (at // 2 + 1) * edge]


def message_kernel(syndrome, region, state, *sides):
    planes, rows, cols = syndrome.shape
    bits = syndrome[...].reshape(planes * rows, cols).astype(F32).astype(BF16)
    column_bits = matmul_nt(one_hot(iota((cols, cols), 0) == iota((cols, cols), 1)), bits).astype(BF16)
    block_rows, block_cols = region.shape
    regions = jnp.concatenate([region[...].astype(F32), jnp.zeros((8 - block_rows, block_cols), F32)])
    spread = one_hot(iota((cols, block_cols), 0) // 2 == iota((cols, block_cols), 1))
    column_region = matmul_nt(spread, regions.astype(BF16)).astype(BF16)
    plane, lane = iota((planes * rows, LANES), 0), iota((planes * rows, LANES), 1)
    ones = jnp.where((iota((cols, LANES), 1) == ONE_LANE) | (iota((cols, LANES), 1) == ONE_LANE + 1), 1.0, 0.0)
    cells = []
    for r in range(rows):
        place = one_hot((plane == lane * rows + r) | (plane == (lane - LOW_LANE) * rows + r))
        region_place = one_hot((iota((8, LANES), 0) == r // 2) & (iota((8, LANES), 1) == REGION_LANE))
        flags = matmul(column_bits, place) + matmul(column_region, region_place) + ones
        cells.append(jnp.concatenate([state[r * cols : (r + 1) * cols].astype(F32), flags], axis=1))
    write_sides(sides, cells, cols)


def fetch(sources, targets, sems):
    copies = [pltpu.make_async_copy(*pair, sems.at[i]) for i, pair in enumerate(zip(sources, targets))]
    for copy in copies:
        copy.start()
    return copies


def prepare_kernel(candidate_bits, gate_bits, bias, embed, bit_weight, spread):
    by_bit = jnp.concatenate([candidate_bits[...], gate_bits[...]], axis=1)
    bias = jnp.concatenate([jnp.zeros_like(bias), bias[...]], axis=1)
    lane = iota((LANES, 1), 0)
    weight = jnp.zeros(bit_weight.shape, F32)
    for part in range(2):
        begin = (0, LOW_LANE)[part]
        for bit in range(2):
            row = two_parts(by_bit[bit : bit + 1])[part].astype(F32)
            here = (lane >= begin) & (lane < begin + 2 * ROUNDS) & (lane % 2 == bit)
            weight = jnp.where(here, row, weight)
        weight = jnp.where(lane == ONE_LANE + part, two_parts(bias)[part].astype(F32), weight)
    bit_weight[...] = weight.astype(BF16)
    for at in range(0, spread.shape[0], embed.shape[0]):
        spread[at : at + embed.shape[0]] = embed[...]


class Patch:
    def __init__(self, cols, state, taps, bits, mask):
        self.cols, self.span, self.width = cols, cols + 2 * HALF, HALF
        self.state, self.taps, self.bits, self.mask = state, taps, bits, mask
        self.groups, self.count = state.shape[:2]
        self.rows, self.channels = self.count // self.span, self.groups * LANES

    def get(self, at):
        return jnp.concatenate([self.state[j, at] for j in range(self.groups)], axis=1)

    def put(self, at, values):
        for j in range(self.groups):
            self.state[j, at] = values[:, j * LANES : (j + 1) * LANES]

    def fill(self, parts, halo, put):
        above, below, left, right, above_left, above_right, below_left, below_right = halo
        parts = (above, *parts, below)
        r = 0
        for part in parts:
            for at in range(0, part.shape[0], self.cols):
                put(pl.ds(r * self.span + self.width, self.cols), part[at : at + self.cols].astype(F32))
                r += 1
        for parts, first in (
            ((above_left, left, below_left), 0),
            ((above_right, right, below_right), self.width + self.cols),
        ):
            values = jnp.concatenate([part[...].astype(F32) for part in parts])
            for r in range(self.rows):
                put(pl.ds(r * self.span + first, self.width), values[r * self.width : (r + 1) * self.width])

    def keep(self, slot, first, values):
        size = values.shape[0]
        mask = self.mask[first : first + size]
        values = jnp.concatenate([values[:, c : c + LANES] * mask for c in range(0, self.channels, LANES)], axis=1)
        for b in range(3):
            moved = values if b == 1 else pltpu.roll(values, 1 if b == 0 else size - 1, 0)
            self.taps[slot, first : first + size, b * self.channels : (b + 1) * self.channels] = moved.astype(BF16)

    def advance(self, first_round, flags, conv, gate_weight, bit_weight):
        span, channels, rows = self.span, self.channels, self.rows
        for first in range(0, rows, rows // 2):
            self.keep(0, first * span, self.get(pl.ds(first * span, rows // 2 * span)))
        lane = iota((1, LANES), 1)
        for step in range(HALF):
            t, slot = first_round + step, step % 2
            now = (lane == 2 * t) | (lane == 2 * t + 1) | (lane == LOW_LANE + 2 * t) | (lane == LOW_LANE + 2 * t + 1)
            self.bits[...] = flags[...] * one_hot(now | (lane >= ONE_LANE))
            total = rows - 2 * (step + 1)
            cut = (total // 4 + total // 2 % 2) * 2
            for begin, part_rows in ((step + 1, cut), (step + 1 + cut, total - cut)):
                first, size = begin * span, part_rows * span
                columns = jnp.concatenate(
                    [self.taps[slot, first + a * span : first + a * span + size] for a in (-1, 0, 1)], axis=1
                )
                flag = self.bits[first : first + size]
                rounded = self.taps[slot, first : first + size, channels : 2 * channels]
                candidate = matmul(columns, conv[...]) + matmul(flag, bit_weight[:, :channels])
                gate = matmul(rounded, gate_weight[...]) + matmul(flag, bit_weight[:, channels:])
                before = self.get(pl.ds(first, size))
                after = before + (0.5 * jnp.tanh(0.5 * gate) + 0.5) * (jnp.tanh(candidate) - before)
                self.put(pl.ds(first, size), after)
                if step < HALF - 1:
                    self.keep(1 - slot, first, after)

    def own(self, r):
        return self.get(pl.ds((self.width + r) * self.span + self.width, self.cols))


def patch_scratch(rows, cols, channels):
    count = (rows + 2 * HALF) * (cols + 2 * HALF)
    return [
        pltpu.VMEM((channels // LANES, count, LANES), F32),
        pltpu.VMEM((2, count, 3 * channels), BF16),
        pltpu.VMEM((count, LANES), BF16),
        pltpu.VMEM((count, LANES), F32),
    ]


def mask_of(flags):
    return matmul(flags, one_hot(iota((LANES, LANES), 0) == ONE_LANE))


def first_kernel(cols, top, bottom, *refs):
    halo, (region, bit_weight, conv_hbm, gate_hbm) = refs[:8], refs[8:12]
    (exact, partial, flags), sides = refs[12:15], refs[15:23]
    state, taps, bits, mask, flags_wide, conv, gate_weight, sems = refs[23:]
    copies = fetch((conv_hbm, gate_hbm), (conv, gate_weight), sems)
    patch = Patch(cols, state, taps, bits, mask)
    channels = patch.channels

    def put(at, values):
        patch.put(at, values[:, :channels])
        flags_wide[at] = values[:, channels:]

    patch.fill((top, bottom), halo, put)
    flags[...] = flags_wide[...].astype(BF16)
    mask[...] = mask_of(flags[...])
    for copy in copies:
        copy.wait()
    patch.advance(0, flags, conv, gate_weight, bit_weight)

    own = patch.rows - 2 * patch.width
    cells = [patch.own(r) for r in range(own)]
    for r in range(own):
        exact[r * cols : (r + 1) * cols] = cells[r]
    write_sides(sides, cells, cols)
    block_cols = cols // 2
    total = jnp.zeros(partial.shape, F32)
    for r in range(0, own, 2):
        begin = (patch.width + r) * patch.span + patch.width
        parts = [
            patch.get(pl.ds(begin + a * patch.span + b, block_cols, stride=2)) for a in range(2) for b in range(2)
        ]
        pooled = (sum(parts[1:], parts[0]) * 0.25).astype(BF16)
        member = one_hot(iota((partial.shape[0], block_cols), 0) == region[r // 2 : r // 2 + 1])
        total = total + matmul(member, pooled)
    partial[...] = total.astype(BF16)


def chunk_kernel(tiles, pieces, out):
    values = pieces[...].astype(F32)
    chunk = values.shape[0] // tiles
    total = values[:chunk]
    for p in range(1, tiles):
        total = total + values[p * chunk : (p + 1) * chunk]
    total = total.astype(BF16)
    for p in range(out.shape[0] // chunk):
        out[p * chunk : (p + 1) * chunk] = total


def second_kernel(
    cols, bands, band_index, exact, above, below, left, right, above_left, above_right, below_left, below_right,
    flags, sums, embed, attn_gain, mlp_gain, bit_weight,
    pool_hbm, key_hbm, value_hbm, query_hbm, out_hbm, up_hbm, down_hbm, return_hbm, conv_hbm, gate_hbm,
    state_out, context_out,
    state, taps, bits, mask, pool_weight, key_weight, value_weight, query_weight, out_weight, up_weight,
    down_weight, return_weight, conv, gate_weight,
    tokens_all, normed_all, keys, values, member, tokens, normed, attention, hidden, context, sems,
):
    copies = fetch(
        (pool_hbm, key_hbm, value_hbm, query_hbm, out_hbm, up_hbm, down_hbm, return_hbm, conv_hbm, gate_hbm),
        (pool_weight, key_weight, value_weight, query_weight, out_weight, up_weight, down_weight, return_weight,
         conv, gate_weight),
        sems,
    )
    patch = Patch(cols, state, taps, bits, mask)
    halo = (above, below, left, right, above_left, above_right, below_left, below_right)
    patch.fill((exact,), halo, patch.put)
    mask[...] = mask_of(flags[...])
    region = matmul(flags[...], one_hot(iota((LANES, LANES), 0) == REGION_LANE))
    member[...] = jnp.where(region == iota(region.shape, 1).astype(F32), 1.0, 0.0)

    band_tokens = sums.shape[0] // bands
    copies[0].wait()
    for band in range(bands):
        at = pl.ds(band * band_tokens, band_tokens)
        total = embed[at].astype(F32) + matmul(sums[at], pool_weight[...])
        tokens_all[at] = total
        normed_all[at] = rms_norm(total, attn_gain[...]).astype(BF16)

    g = band_index[0]
    own = pl.ds(pl.multiple_of(g * band_tokens, band_tokens), band_tokens)
    tokens[:band_tokens] = tokens_all[own]
    normed[:band_tokens] = normed_all[own]
    blocks = patch.span // 2
    room = (blocks + 7) // 8 * 8
    block_rows = patch.width // 2
    side = room * block_rows
    for number, (band, row) in enumerate(
        ((jnp.maximum(g - 1, 0), 0), (jnp.minimum(g + 1, bands - 1), patch.rows - patch.width))
    ):
        pick = jnp.concatenate(
            [member[pl.ds((row + 2 * r) * patch.span, room, stride=2)] for r in range(block_rows)]
        ).astype(BF16)
        at = pl.ds(pl.multiple_of(band * band_tokens, band_tokens), band_tokens)
        into = pl.ds(band_tokens + number * side, side)
        tokens[into] = select(pick, tokens_all[at])
        normed[into] = matmul(pick, normed_all[at]).astype(BF16)

    copies[1].wait()
    keys[...] = matmul(normed_all[...], key_weight[...]).astype(BF16)
    copies[2].wait()
    values[...] = matmul(normed_all[...], value_weight[...]).astype(BF16)
    copies[3].wait()
    queries = matmul(normed[...], query_weight[...]).astype(BF16)
    for head in range(HEADS):
        at = slice(head * HDIM, (head + 1) * HDIM)
        scores = matmul_nt(queries[:, at], keys[:, at]) * (1.0 / math.sqrt(HDIM))
        weights = jnp.exp(scores - jnp.max(scores, axis=-1, keepdims=True))
        denominator = jnp.sum(weights, axis=-1, keepdims=True)
        attention[:, at] = (matmul(weights.astype(BF16), values[:, at]) / denominator).astype(BF16)
    copies[4].wait()
    attended = tokens[...] + matmul(attention[...], out_weight[...])
    tokens[...] = attended
    normed[...] = rms_norm(attended, mlp_gain[...]).astype(BF16)
    copies[5].wait()
    part = 512
    for at in range(0, up_weight.shape[1], part):
        hidden[:, at : at + part] = jax.nn.gelu(matmul(normed[...], up_weight[:, at : at + part])).astype(BF16)
    copies[6].wait()
    context[...] = (tokens[...] + matmul(hidden[...], down_weight[...])).astype(BF16)
    context_out[...] = context[:band_tokens]
    copies[7].wait()
    returned = matmul(context[...], return_weight[...])

    first, last = patch.width * patch.span, (patch.rows - patch.width) * patch.span
    middle = pl.ds(first, last - first)
    patch.put(middle, patch.get(middle) + select(member[first:last].astype(BF16), returned[:band_tokens]))
    for number, row in enumerate((0, patch.rows - patch.width)):
        for r in range(patch.width):
            start = band_tokens + number * side + r // 2 * room
            share = returned[start : start + blocks]
            for c in range(2):
                at = pl.ds((row + r) * patch.span + c, blocks, stride=2)
                patch.put(at, patch.get(at) + share)

    copies[8].wait()
    copies[9].wait()
    patch.advance(HALF, flags, conv, gate_weight, bit_weight)
    for r in range(patch.rows - 2 * patch.width):
        state_out[r * cols : (r + 1) * cols] = patch.own(r).astype(BF16)


def local(
    syndrome_bits, region_assign, state_in, bit_to_candidate, bit_to_gate, conv_weight, gate_weight, gate_bias,
    pool_weight, region_embed, attn_norm_gain, query_weight, key_weight, value_weight, out_weight, mlp_norm_gain,
    mlp_up, mlp_down, return_weight,
):
    rows, cols, channels = state_in.shape
    band_tokens, embed_width = region_embed.shape
    bands, tiles = lax.axis_size("ctx"), lax.axis_size("tile")
    conv = conv_weight.reshape(9 * channels, channels)
    half = HALF * cols

    sides = call(
        message_kernel,
        "message",
        (syndrome_bits.reshape(2 * ROUNDS, rows, cols), region_assign, state_in.reshape(rows * cols, channels)),
        side_arrays(half, channels + LANES),
    )
    halo = exchange(sides)
    embed, _ = lax.optimization_barrier((region_embed, sides[0]))
    bit_weight, embed = call(
        prepare_kernel,
        "prepare",
        (bit_to_candidate, bit_to_gate, gate_bias[None], embed),
        [array(LANES, 2 * channels, BF16), array(bands * band_tokens, embed_width, BF16)],
        moved=8 * MIB,
    )
    embed, *rows_halo = lax.optimization_barrier((embed, *halo[:2]))
    halo = (*rows_halo, *halo[2:])
    embed = lax.all_to_all(embed.reshape(bands, band_tokens, -1), "ctx", 0, 0).reshape(-1, embed_width)

    count = (rows + 2 * HALF) * (cols + 2 * HALF)
    flops = 15 * rows * cols * HALF * 2 * channels * channels
    exact, partial, flags, *new_sides = call(
        functools.partial(first_kernel, cols),
        "rounds",
        (*sides[:2], *halo, region_assign, bit_weight, conv, gate_weight),
        [array(rows * cols, channels, F32), array(band_tokens, channels, BF16), array(count, LANES, BF16)]
        + side_arrays(half, channels),
        patch_scratch(rows, cols, channels)
        + [
            pltpu.VMEM((count, LANES), F32), pltpu.VMEM(conv.shape, BF16), pltpu.VMEM(gate_weight.shape, BF16),
            pltpu.SemaphoreType.DMA((2,)),
        ],
        in_hbm=(12, 13),
        flops=flops,
    )

    partial, embed = lax.optimization_barrier((partial, embed))
    pieces = lax.all_to_all(partial.reshape(tiles, -1, channels), "tile", 0, 0)
    (chunks,) = call(
        functools.partial(chunk_kernel, tiles),
        "chunk",
        (pieces.reshape(band_tokens, channels),),
        [array(bands * band_tokens, channels, BF16)],
        grant=8,
    )
    sums = lax.all_to_all(chunks.reshape(bands * tiles, -1, channels), ("ctx", "tile"), 0, 0)
    halo = exchange(new_sides)

    layer = (
        pool_weight, key_weight, value_weight, query_weight, out_weight, mlp_up, mlp_down, return_weight, conv,
        gate_weight,
    )
    blocks = (cols + 2 * HALF) // 2
    layer_rows = band_tokens + HALF * ((blocks + 7) // 8 * 8)
    all_tokens = bands * band_tokens
    state, context = call(
        functools.partial(second_kernel, cols, bands),
        "context",
        (
            lax.axis_index("ctx").reshape(1), exact, *halo, flags, sums.reshape(all_tokens, channels), embed,
            attn_norm_gain[None], mlp_norm_gain[None], bit_weight, *layer,
        ),
        [array(rows * cols, channels, BF16), array(band_tokens, embed_width, BF16)],
        patch_scratch(rows, cols, channels)
        + [pltpu.VMEM(weight.shape, BF16) for weight in layer]
        + [
            pltpu.VMEM((all_tokens, embed_width), F32), pltpu.VMEM((all_tokens, embed_width), BF16),
            pltpu.VMEM((all_tokens, embed_width), BF16), pltpu.VMEM((all_tokens, embed_width), BF16),
            pltpu.VMEM((count, LANES), F32),
            pltpu.VMEM((layer_rows, embed_width), F32), pltpu.VMEM((layer_rows, embed_width), BF16),
            pltpu.VMEM((layer_rows, embed_width), BF16), pltpu.VMEM((layer_rows, mlp_up.shape[1]), BF16),
            pltpu.VMEM((layer_rows, embed_width), BF16), pltpu.SemaphoreType.DMA((len(layer),)),
        ],
        in_hbm=range(16, 16 + len(layer)),
        scalars=(0,),
        flops=2 * flops,
    )
    return (state.reshape(rows, cols, channels), context)


def solution(mesh):
    return jax.shard_map(
        local,
        mesh=mesh,
        in_specs=(
            P(None, None, "ctx", "tile"),
            P("ctx", "tile"),
            P("ctx", "tile", None),
            P(), P(), P(), P(), P(), P(),
            P("ctx", None),
            P(), P(), P(), P(), P(), P(), P(), P(), P(),
        ),
        out_specs=(P("ctx", "tile", None), P("ctx", None)),
        check_vma=False,
    )
```

profile of v0, /device:TPU:0, one launch (start us, length us, event | category | flops | bytes accessed | tf_op | source)
XLA Modules:
  0.0 125.8 jit_solution(10612364097792286592)
XLA Ops:
  0.6 2.1 %message.1 = (bf16[128,640]{1,0:T(8,128)(2,1)}, bf16[128,640]{1,0:T(8,128)(2,1)}, bf16[32,640]{1,0:T(8,128)(2,1)}, bf16[32,640]{1,0:T(8,128)(2,1)}, bf16[16,640]...) custom-call(s32[16,8,32]{2,1,0:T(8,128)} %bitcast.20, ...), custom_call_target="tpu_custom_call" | custom-call | bytes 1048576 | tf_op jit(solution)/shard_map/message/pallas_call | solution.py:84
  2.7 5.0 %collective-permute-start = (bf16[128,640]{1,0:T(8,128)(2,1)}, bf16[128,640]{1,0:T(8,128)(2,1)S(1)}, u32[]{:S(2)}, u32[]{:S(2)}) collective-permute-start(bf16[128,640]{1,0:T(8,128)(2,1)} %get-tuple-element.32.bottom), channel_id=1, source_target_pairs={{0,8},{1,9},{2,10},{3,11},{4,12},{5,13},{6,14},{7,15},{8,16},{9,17... | collective-permute-start | bytes 491528 | tf_op jit(solution)/shard_map/ppermute | solution.py:31
  7.7 1.3 %collective-permute-start.1 = (bf16[128,640]{1,0:T(8,128)(2,1)}, bf16[128,640]{1,0:T(8,128)(2,1)S(1)}, u32[]{:S(2)}, u32[]{:S(2)}) collective-permute-start(bf16[128,640]{1,0:T(8,128)(2,1)} %get-tuple-element.31.top), channel_id=1, source_target_pairs={{8,0},{9,1},{10,2},{11,3},{12,4},{13,5},{14,6},{15,7},{16,8},{17,9... | collective-permute-start | bytes 491528 | tf_op jit(solution)/shard_map/ppermute | solution.py:31
  9.0 3.4 %collective-permute-start.4 = (bf16[16,640]{1,0:T(8,128)(2,1)}, bf16[16,640]{1,0:T(8,128)(2,1)S(1)}, u32[]{:S(2)}, u32[]{:S(2)}) collective-permute-start(bf16[16,640]{1,0:T(8,128)(2,1)} %get-tuple-element.39), channel_id=1, source_target_pairs={{0,9},{1,10},{2,11},{3,12},{4,13},{5,14},{6,15},{8,17},{9,18},{10,... | collective-permute-start | bytes 61448 | tf_op jit(solution)/shard_map/ppermute | solution.py:31
  12.5 4.2 %collective-permute-start.2 = (bf16[32,640]{1,0:T(8,128)(2,1)}, bf16[32,640]{1,0:T(8,128)(2,1)S(1)}, u32[]{:S(2)}, u32[]{:S(2)}) collective-permute-start(bf16[32,640]{1,0:T(8,128)(2,1)} %get-tuple-element.37), channel_id=1, source_target_pairs={{0,1},{1,2},{2,3},{3,4},{4,5},{5,6},{6,7},{8,9},{9,10},{10,11},{11... | collective-permute-start | bytes 122888 | tf_op jit(solution)/shard_map/ppermute | solution.py:31
  16.6 1.3 %collective-permute-start.3 = (bf16[32,640]{1,0:T(8,128)(2,1)}, bf16[32,640]{1,0:T(8,128)(2,1)S(1)}, u32[]{:S(2)}, u32[]{:S(2)}) collective-permute-start(bf16[32,640]{1,0:T(8,128)(2,1)} %get-tuple-element.38), channel_id=1, source_target_pairs={{1,0},{2,1},{3,2},{4,3},{5,4},{6,5},{7,6},{9,8},{10,9},{11,10},{12... | collective-permute-start | bytes 122888 | tf_op jit(solution)/shard_map/ppermute | solution.py:31
  17.9 2.1 %prepare.1 = (bf16[128,1024]{1,0:T(8,128)(2,1)}, bf16[512,1024]{1,0:T(8,128)(2,1)}) custom-call(f32[2,512]{1,0:T(2,128)} %candidate_bits.1, f32[2,512]{1,0:T(2,128)} %gate_bits.1, f32[1,512]{1,0:T(1,128)} %bitcast.21, bf16[128,1024]{1,0:T(8,128)(2,1)} %embed), custom_call_target="tpu_custom_call" | custom-call | bytes 8388608 | tf_op jit(solution)/shard_map/prepare/pallas_call | solution.py:84
  20.1 0.0 collective-permute-done.refs_0_
  20.1 0.0 collective-permute-done.1.refs_1_
  20.1 0.0 copy-start.3
  20.1 3.7 %all-to-all-start = ((bf16[4,128,1024]{2,1,0:T(8,128)(2,1)}), bf16[4,128,1024]{2,1,0:T(8,128)(2,1)S(1)}, u32[]{:S(2)}, u32[]{:S(2)}) async-start(bf16[4,128,1024]{2,1,0:T(8,128)(2,1)} %bitcast.16), calls=%async_computation | async-start | bytes 2097152 | tf_op jit(solution)/shard_map/all_to_all | solution.py:413
  23.8 0.0 copy-done.13
  23.8 0.7 collective-permute-start.5
  24.4 0.0 copy-done.12
  24.4 0.7 collective-permute-start.6
  25.1 0.0 collective-permute-done.4.refs_4_
  25.1 0.0 copy-start.10
  25.1 0.0 copy-done.11
  25.1 1.3 %collective-permute-start.7 = (bf16[16,640]{1,0:T(8,128)(2,1)S(1)}, bf16[16,640]{1,0:T(8,128)(2,1)S(1)}, u32[]{:S(2)}, u32[]{:S(2)}) collective-permute-start(bf16[16,640]{1,0:T(8,128)(2,1)S(1)} %copy-done.11), channel_id=1, source_target_pairs={{9,0},{10,1},{11,2},{12,3},{13,4},{14,5},{15,6},{17,8},{18,9},{19,... | collective-permute-start | bytes 61448 | tf_op jit(solution)/shard_map/ppermute | solution.py:31
  26.4 0.0 collective-permute-done.5.refs_5_
  26.5 0.0 copy-start.14
  26.5 0.0 collective-permute-done.6.refs_6_
  26.5 0.0 copy-start.15
  26.5 13.6 %collective-permute-done.7.refs_7_ = bf16[16,640]{1,0:T(8,128)(2,1)S(1)} collective-permute-done((bf16[16,640]{1,0:T(8,128)(2,1)S(1)}, bf16[16,640]{1,0:T(8,128)(2,1)S(1)}, u32[]{:S(2)}, u32[]{:S(2)}) %collective-permute-start.7) | collective-permute-done | bytes 20512 | tf_op jit(solution)/shard_map/ppermute | solution.py:31
  40.1 0.0 collective-permute-done.2.refs_2_
  40.1 0.0 collective-permute-done.3.refs_3_
  40.1 0.0 copy-start.7
  40.1 0.0 copy-done.2
  40.1 0.0 copy-done.3
  40.2 0.5 copy-done.16
  40.7 0.0 copy-done.6
  40.7 0.0 copy-done.7
  40.7 15.9 %rounds.1 = (f32[256,512]{1,0:T(8,128)}, bf16[128,512]{1,0:T(8,128)(2,1)}, bf16[640,128]{1,0:T(8,128)(2,1)}, bf16[128,512]{1,0:T(8,128)(2,1)}, bf16[128,512]{1,0...) custom-call(bf16[128,640]{1,0:T(8,128)(2,1)} %get-tuple-element.31.t, ...), custom_call_target="tpu_custom_call" | custom-call | flops 8053063680 | bytes 1048576 | tf_op jit(solution)/shard_map/rounds/pallas_call | solution.py:84
  56.6 0.0 all-to-all-done
  56.6 0.0 copy-start
  56.7 11.3 %all_to_all.15 = bf16[8,16,512]{2,1,0:T(8,128)(2,1)S(1)} all-to-all(bf16[8,16,512]{2,1,0:T(8,128)(2,1)} %bitcast.19), channel_id=1, replica_groups=mesh['ctx'=4,'tile'=8] {'tile'}, dimensions={0} | all-to-all | bytes 262144 | tf_op jit(solution)/shard_map/all_to_all | solution.py:433
  67.9 0.9 chunk.1
  68.8 2.6 %all-to-all-start.2 = ((bf16[32,16,512]{2,1,0:T(8,128)(2,1)}), bf16[32,16,512]{2,1,0:T(8,128)(2,1)S(1)}, u32[]{:S(2)}, u32[]{:S(2)}) async-start(bf16[32,16,512]{2,1,0:T(8,128)(2,1)} %bitcast.9), calls=%async_computation.2 | async-start | bytes 1048576 | tf_op jit(solution)/shard_map/all_to_all | solution.py:441
  71.4 3.5 %collective-permute-start.8 = (bf16[128,512]{1,0:T(8,128)(2,1)}, bf16[128,512]{1,0:T(8,128)(2,1)S(1)}, u32[]{:S(2)}, u32[]{:S(2)}) collective-permute-start(bf16[128,512]{1,0:T(8,128)(2,1)} %get-tuple-element.45), channel_id=1, source_target_pairs={{0,8},{1,9},{2,10},{3,11},{4,12},{5,13},{6,14},{7,15},{8,16},{9,17... | collective-permute-start | bytes 393224 | tf_op jit(solution)/shard_map/ppermute | solution.py:31
  75.0 1.3 %collective-permute-start.9 = (bf16[128,512]{1,0:T(8,128)(2,1)}, bf16[128,512]{1,0:T(8,128)(2,1)S(1)}, u32[]{:S(2)}, u32[]{:S(2)}) collective-permute-start(bf16[128,512]{1,0:T(8,128)(2,1)} %get-tuple-element.46), channel_id=1, source_target_pairs={{8,0},{9,1},{10,2},{11,3},{12,4},{13,5},{14,6},{15,7},{16,8},{17,9... | collective-permute-start | bytes 393224 | tf_op jit(solution)/shard_map/ppermute | solution.py:31
  76.3 3.7 %collective-permute-start.12 = (bf16[16,512]{1,0:T(8,128)(2,1)}, bf16[16,512]{1,0:T(8,128)(2,1)S(1)}, u32[]{:S(2)}, u32[]{:S(2)}) collective-permute-start(bf16[16,512]{1,0:T(8,128)(2,1)} %get-tuple-element.49), channel_id=1, source_target_pairs={{0,9},{1,10},{2,11},{3,12},{4,13},{5,14},{6,15},{8,17},{9,18},{10,... | collective-permute-start | bytes 49160 | tf_op jit(solution)/shard_map/ppermute | solution.py:31
  80.0 0.7 collective-permute-start.13
  80.7 0.7 collective-permute-start.14
  81.4 0.3 collective-permute-done.12.above_left
  81.7 6.0 %collective-permute-start.10 = (bf16[32,512]{1,0:T(8,128)(2,1)}, bf16[32,512]{1,0:T(8,128)(2,1)S(1)}, u32[]{:S(2)}, u32[]{:S(2)}) collective-permute-start(bf16[32,512]{1,0:T(8,128)(2,1)} %get-tuple-element.47), channel_id=1, source_target_pairs={{0,1},{1,2},{2,3},{3,4},{4,5},{5,6},{6,7},{8,9},{9,10},{10,11},{11... | collective-permute-start | bytes 98312 | tf_op jit(solution)/shard_map/ppermute | solution.py:31
  87.7 0.0 collective-permute-done.13.above_right
  87.7 0.0 copy-start.18
  87.7 1.3 %collective-permute-start.11 = (bf16[32,512]{1,0:T(8,128)(2,1)}, bf16[32,512]{1,0:T(8,128)(2,1)S(1)}, u32[]{:S(2)}, u32[]{:S(2)}) collective-permute-start(bf16[32,512]{1,0:T(8,128)(2,1)} %get-tuple-element.48), channel_id=1, source_target_pairs={{1,0},{2,1},{3,2},{4,3},{5,4},{6,5},{7,6},{9,8},{10,9},{11,10},{12... | collective-permute-start | bytes 98312 | tf_op jit(solution)/shard_map/ppermute | solution.py:31
  89.0 0.0 collective-permute-done.14.below_left
  89.0 1.5 %collective-permute-start.15 = (bf16[16,512]{1,0:T(8,128)(2,1)}, bf16[16,512]{1,0:T(8,128)(2,1)S(1)}, u32[]{:S(2)}, u32[]{:S(2)}) collective-permute-start(bf16[16,512]{1,0:T(8,128)(2,1)} %get-tuple-element.52), channel_id=1, source_target_pairs={{9,0},{10,1},{11,2},{12,3},{13,4},{14,5},{15,6},{17,8},{18,9},{19,... | collective-permute-start | bytes 49160 | tf_op jit(solution)/shard_map/ppermute | solution.py:31
  90.5 7.8 %collective-permute-done.15.below_right = bf16[16,512]{1,0:T(8,128)(2,1)S(1)} collective-permute-done((bf16[16,512]{1,0:T(8,128)(2,1)}, bf16[16,512]{1,0:T(8,128)(2,1)S(1)}, u32[]{:S(2)}, u32[]{:S(2)}) %collective-permute-start.15) | collective-permute-done | bytes 16416 | tf_op jit(solution)/shard_map/ppermute | solution.py:31
  98.3 0.0 collective-permute-done.10.left
  98.3 0.0 collective-permute-done.11.right
  98.3 0.0 collective-permute-done.8.above
  98.3 0.0 copy-start.4
  98.4 0.0 collective-permute-done.9.below
  98.4 0.0 all-to-all-done.2
  98.4 0.5 copy-done.20
  98.9 0.0 copy-done.8
  98.9 0.0 copy-done.9
  98.9 0.1 copy-done.4
  99.0 0.1 copy-done.5
  99.1 0.2 copy-done.1
  99.2 26.3 %context.1 = (bf16[256,512]{1,0:T(8,128)(2,1)}, bf16[128,1024]{1,0:T(8,128)(2,1)}) custom-call(s32[1]{0:T(128)} %bitcast.band_index, f32[256,512]{1,0:T(8,128)} %get-tuple-element.44.exact, bf16[128,512]{1,0:T(8,128)(2,1)} %copy-done.4, bf16[128,512]{1,0:T(8,128)(2,1)} %copy-done.5, bf16[32,512]{1,0:T(8,128)(2,1)} %copy-done.8, bf16[32,512]{1,0:T(8,128)(2,1)} %copy-done.9, ...), custom_call_target="tpu_custom_call" | custom-call | flops 16106127360 | bytes 1048576 | tf_op jit(solution)/shard_map/context/pallas_call | solution.py:84
  (20 shorter events, 0.0 us)
Async XLA Ops:
  2.7 21.0 %copy-start.13 = (bf16[16,640]{1,0:T(8,128)(2,1)S(1)}, bf16[16,640]{1,0:T(8,128)(2,1)}, u32[]{:S(2)}) copy-start(bf16[16,640]{1,0:T(8,128)(2,1)} %get-tuple-element.40) | copy-start | bytes 61444
  2.7 21.7 %copy-start.12 = (bf16[16,640]{1,0:T(8,128)(2,1)S(1)}, bf16[16,640]{1,0:T(8,128)(2,1)}, u32[]{:S(2)}) copy-start(bf16[16,640]{1,0:T(8,128)(2,1)} %get-tuple-element.41) | copy-start | bytes 61444
  2.7 22.4 %copy-start.11 = (bf16[16,640]{1,0:T(8,128)(2,1)S(1)}, bf16[16,640]{1,0:T(8,128)(2,1)}, u32[]{:S(2)}) copy-start(bf16[16,640]{1,0:T(8,128)(2,1)} %get-tuple-element.42) | copy-start | bytes 61444
  2.7 17.3 %collective-permute-start = (bf16[128,640]{1,0:T(8,128)(2,1)}, bf16[128,640]{1,0:T(8,128)(2,1)S(1)}, u32[]{:S(2)}, u32[]{:S(2)}) collective-permute-start(bf16[128,640]{1,0:T(8,128)(2,1)} %get-tuple-element.32.bottom), channel_id=1, source_target_pairs={{0,8},{1,9},{2,10},{3,11},{4,12},{5,13},{6,14},{7,15},{8,16},{9,17... | collective-permute-start | bytes 491528 | tf_op jit(solution)/shard_map/ppermute | solution.py:31
  7.7 12.4 %collective-permute-start.1 = (bf16[128,640]{1,0:T(8,128)(2,1)}, bf16[128,640]{1,0:T(8,128)(2,1)S(1)}, u32[]{:S(2)}, u32[]{:S(2)}) collective-permute-start(bf16[128,640]{1,0:T(8,128)(2,1)} %get-tuple-element.31.top), channel_id=1, source_target_pairs={{8,0},{9,1},{10,2},{11,3},{12,4},{13,5},{14,6},{15,7},{16,8},{17,9... | collective-permute-start | bytes 491528 | tf_op jit(solution)/shard_map/ppermute | solution.py:31
  9.0 16.1 %collective-permute-start.4 = (bf16[16,640]{1,0:T(8,128)(2,1)}, bf16[16,640]{1,0:T(8,128)(2,1)S(1)}, u32[]{:S(2)}, u32[]{:S(2)}) collective-permute-start(bf16[16,640]{1,0:T(8,128)(2,1)} %get-tuple-element.39), channel_id=1, source_target_pairs={{0,9},{1,10},{2,11},{3,12},{4,13},{5,14},{6,15},{8,17},{9,18},{10,... | collective-permute-start | bytes 61448 | tf_op jit(solution)/shard_map/ppermute | solution.py:31
  12.5 27.7 %collective-permute-start.2 = (bf16[32,640]{1,0:T(8,128)(2,1)}, bf16[32,640]{1,0:T(8,128)(2,1)S(1)}, u32[]{:S(2)}, u32[]{:S(2)}) collective-permute-start(bf16[32,640]{1,0:T(8,128)(2,1)} %get-tuple-element.37), channel_id=1, source_target_pairs={{0,1},{1,2},{2,3},{3,4},{4,5},{5,6},{6,7},{8,9},{9,10},{10,11},{11... | collective-permute-start | bytes 122888 | tf_op jit(solution)/shard_map/ppermute | solution.py:31
  16.6 23.5 %collective-permute-start.3 = (bf16[32,640]{1,0:T(8,128)(2,1)}, bf16[32,640]{1,0:T(8,128)(2,1)S(1)}, u32[]{:S(2)}, u32[]{:S(2)}) collective-permute-start(bf16[32,640]{1,0:T(8,128)(2,1)} %get-tuple-element.38), channel_id=1, source_target_pairs={{1,0},{2,1},{3,2},{4,3},{5,4},{6,5},{7,6},{9,8},{10,9},{11,10},{12... | collective-permute-start | bytes 122888 | tf_op jit(solution)/shard_map/ppermute | solution.py:31
  20.1 20.1 %copy-start.2 = (bf16[128,640]{1,0:T(8,128)(2,1)}, bf16[128,640]{1,0:T(8,128)(2,1)S(1)}, u32[]{:S(2)}) copy-start(bf16[128,640]{1,0:T(8,128)(2,1)S(1)} %collective-permute-done.refs_0_) | copy-start | bytes 491524
  20.1 20.1 %copy-start.3 = (bf16[128,640]{1,0:T(8,128)(2,1)}, bf16[128,640]{1,0:T(8,128)(2,1)S(1)}, u32[]{:S(2)}) copy-start(bf16[128,640]{1,0:T(8,128)(2,1)S(1)} %collective-permute-done.1.refs_1_) | copy-start | bytes 491524
  20.1 36.5 %all-to-all-start = ((bf16[4,128,1024]{2,1,0:T(8,128)(2,1)}), bf16[4,128,1024]{2,1,0:T(8,128)(2,1)S(1)}, u32[]{:S(2)}, u32[]{:S(2)}) async-start(bf16[4,128,1024]{2,1,0:T(8,128)(2,1)} %bitcast.16), calls=%async_computation | async-start | bytes 2097152 | tf_op jit(solution)/shard_map/all_to_all | solution.py:413
  23.8 2.7 %collective-permute-start.5 = (bf16[16,640]{1,0:T(8,128)(2,1)S(1)}, bf16[16,640]{1,0:T(8,128)(2,1)S(1)}, u32[]{:S(2)}, u32[]{:S(2)}) collective-permute-start(bf16[16,640]{1,0:T(8,128)(2,1)S(1)} %copy-done.13), channel_id=1, source_target_pairs={{1,8},{2,9},{3,10},{4,11},{5,12},{6,13},{7,14},{9,16},{10,17},{11,... | collective-permute-start | bytes 61448 | tf_op jit(solution)/shard_map/ppermute | solution.py:31
  24.4 2.0 %collective-permute-start.6 = (bf16[16,640]{1,0:T(8,128)(2,1)S(1)}, bf16[16,640]{1,0:T(8,128)(2,1)S(1)}, u32[]{:S(2)}, u32[]{:S(2)}) collective-permute-start(bf16[16,640]{1,0:T(8,128)(2,1)S(1)} %copy-done.12), channel_id=1, source_target_pairs={{8,1},{9,2},{10,3},{11,4},{12,5},{13,6},{14,7},{16,9},{17,10},{18,... | collective-permute-start | bytes 61448 | tf_op jit(solution)/shard_map/ppermute | solution.py:31
  25.1 15.0 %copy-start.10 = (bf16[16,640]{1,0:T(8,128)(2,1)}, bf16[16,640]{1,0:T(8,128)(2,1)S(1)}, u32[]{:S(2)}) copy-start(bf16[16,640]{1,0:T(8,128)(2,1)S(1)} %collective-permute-done.4.refs_4_) | copy-start | bytes 61444
  25.1 15.0 %collective-permute-start.7 = (bf16[16,640]{1,0:T(8,128)(2,1)S(1)}, bf16[16,640]{1,0:T(8,128)(2,1)S(1)}, u32[]{:S(2)}, u32[]{:S(2)}) collective-permute-start(bf16[16,640]{1,0:T(8,128)(2,1)S(1)} %copy-done.11), channel_id=1, source_target_pairs={{9,0},{10,1},{11,2},{12,3},{13,4},{14,5},{15,6},{17,8},{18,9},{19,... | collective-permute-start | bytes 61448 | tf_op jit(solution)/shard_map/ppermute | solution.py:31
  26.5 13.7 %copy-start.14 = (bf16[16,640]{1,0:T(8,128)(2,1)}, bf16[16,640]{1,0:T(8,128)(2,1)S(1)}, u32[]{:S(2)}) copy-start(bf16[16,640]{1,0:T(8,128)(2,1)S(1)} %collective-permute-done.5.refs_5_) | copy-start | bytes 61444
  26.5 13.7 %copy-start.15 = (bf16[16,640]{1,0:T(8,128)(2,1)}, bf16[16,640]{1,0:T(8,128)(2,1)S(1)}, u32[]{:S(2)}) copy-start(bf16[16,640]{1,0:T(8,128)(2,1)S(1)} %collective-permute-done.6.refs_6_) | copy-start | bytes 61444
  40.1 0.6 copy-start.16
  40.1 0.6 copy-start.6
  40.1 0.6 copy-start.7
  56.6 41.8 %copy-start = (bf16[4,128,1024]{2,1,0:T(8,128)(2,1)}, bf16[4,128,1024]{2,1,0:T(8,128)(2,1)S(1)}, u32[]{:S(2)}) copy-start(bf16[4,128,1024]{2,1,0:T(8,128)(2,1)S(1)} %all-to-all-done) | copy-start | bytes 3145732
  68.8 29.6 %all-to-all-start.2 = ((bf16[32,16,512]{2,1,0:T(8,128)(2,1)}), bf16[32,16,512]{2,1,0:T(8,128)(2,1)S(1)}, u32[]{:S(2)}, u32[]{:S(2)}) async-start(bf16[32,16,512]{2,1,0:T(8,128)(2,1)} %bitcast.9), calls=%async_computation.2 | async-start | bytes 1048576 | tf_op jit(solution)/shard_map/all_to_all | solution.py:441
  71.4 26.9 %collective-permute-start.8 = (bf16[128,512]{1,0:T(8,128)(2,1)}, bf16[128,512]{1,0:T(8,128)(2,1)S(1)}, u32[]{:S(2)}, u32[]{:S(2)}) collective-permute-start(bf16[128,512]{1,0:T(8,128)(2,1)} %get-tuple-element.45), channel_id=1, source_target_pairs={{0,8},{1,9},{2,10},{3,11},{4,12},{5,13},{6,14},{7,15},{8,16},{9,17... | collective-permute-start | bytes 393224 | tf_op jit(solution)/shard_map/ppermute | solution.py:31
  75.0 23.4 %collective-permute-start.9 = (bf16[128,512]{1,0:T(8,128)(2,1)}, bf16[128,512]{1,0:T(8,128)(2,1)S(1)}, u32[]{:S(2)}, u32[]{:S(2)}) collective-permute-start(bf16[128,512]{1,0:T(8,128)(2,1)} %get-tuple-element.46), channel_id=1, source_target_pairs={{8,0},{9,1},{10,2},{11,3},{12,4},{13,5},{14,6},{15,7},{16,8},{17,9... | collective-permute-start | bytes 393224 | tf_op jit(solution)/shard_map/ppermute | solution.py:31
  76.3 5.4 %collective-permute-start.12 = (bf16[16,512]{1,0:T(8,128)(2,1)}, bf16[16,512]{1,0:T(8,128)(2,1)S(1)}, u32[]{:S(2)}, u32[]{:S(2)}) collective-permute-start(bf16[16,512]{1,0:T(8,128)(2,1)} %get-tuple-element.49), channel_id=1, source_target_pairs={{0,9},{1,10},{2,11},{3,12},{4,13},{5,14},{6,15},{8,17},{9,18},{10,... | collective-permute-start | bytes 49160 | tf_op jit(solution)/shard_map/ppermute | solution.py:31
  80.0 7.6 %collective-permute-start.13 = (bf16[16,512]{1,0:T(8,128)(2,1)}, bf16[16,512]{1,0:T(8,128)(2,1)S(1)}, u32[]{:S(2)}, u32[]{:S(2)}) collective-permute-start(bf16[16,512]{1,0:T(8,128)(2,1)} %get-tuple-element.50), channel_id=1, source_target_pairs={{1,8},{2,9},{3,10},{4,11},{5,12},{6,13},{7,14},{9,16},{10,17},{11,... | collective-permute-start | bytes 49160 | tf_op jit(solution)/shard_map/ppermute | solution.py:31
  80.7 8.3 %collective-permute-start.14 = (bf16[16,512]{1,0:T(8,128)(2,1)}, bf16[16,512]{1,0:T(8,128)(2,1)S(1)}, u32[]{:S(2)}, u32[]{:S(2)}) collective-permute-start(bf16[16,512]{1,0:T(8,128)(2,1)} %get-tuple-element.51), channel_id=1, source_target_pairs={{8,1},{9,2},{10,3},{11,4},{12,5},{13,6},{14,7},{16,9},{17,10},{18,... | collective-permute-start | bytes 49160 | tf_op jit(solution)/shard_map/ppermute | solution.py:31
  81.7 16.7 %copy-start.17 = (bf16[16,512]{1,0:T(8,128)(2,1)}, bf16[16,512]{1,0:T(8,128)(2,1)S(1)}, u32[]{:S(2)}) copy-start(bf16[16,512]{1,0:T(8,128)(2,1)S(1)} %collective-permute-done.12.above_left) | copy-start | bytes 49156
  81.7 16.6 %collective-permute-start.10 = (bf16[32,512]{1,0:T(8,128)(2,1)}, bf16[32,512]{1,0:T(8,128)(2,1)S(1)}, u32[]{:S(2)}, u32[]{:S(2)}) collective-permute-start(bf16[32,512]{1,0:T(8,128)(2,1)} %get-tuple-element.47), channel_id=1, source_target_pairs={{0,1},{1,2},{2,3},{3,4},{4,5},{5,6},{6,7},{8,9},{9,10},{10,11},{11... | collective-permute-start | bytes 98312 | tf_op jit(solution)/shard_map/ppermute | solution.py:31
  87.7 10.7 %copy-start.18 = (bf16[16,512]{1,0:T(8,128)(2,1)}, bf16[16,512]{1,0:T(8,128)(2,1)S(1)}, u32[]{:S(2)}) copy-start(bf16[16,512]{1,0:T(8,128)(2,1)S(1)} %collective-permute-done.13.above_right) | copy-start | bytes 49156
  87.7 10.6 %collective-permute-start.11 = (bf16[32,512]{1,0:T(8,128)(2,1)}, bf16[32,512]{1,0:T(8,128)(2,1)S(1)}, u32[]{:S(2)}, u32[]{:S(2)}) collective-permute-start(bf16[32,512]{1,0:T(8,128)(2,1)} %get-tuple-element.48), channel_id=1, source_target_pairs={{1,0},{2,1},{3,2},{4,3},{5,4},{6,5},{7,6},{9,8},{10,9},{11,10},{12... | collective-permute-start | bytes 98312 | tf_op jit(solution)/shard_map/ppermute | solution.py:31
  89.0 9.4 %copy-start.19 = (bf16[16,512]{1,0:T(8,128)(2,1)}, bf16[16,512]{1,0:T(8,128)(2,1)S(1)}, u32[]{:S(2)}) copy-start(bf16[16,512]{1,0:T(8,128)(2,1)S(1)} %collective-permute-done.14.below_left) | copy-start | bytes 49156
  89.0 9.3 %collective-permute-start.15 = (bf16[16,512]{1,0:T(8,128)(2,1)}, bf16[16,512]{1,0:T(8,128)(2,1)S(1)}, u32[]{:S(2)}, u32[]{:S(2)}) collective-permute-start(bf16[16,512]{1,0:T(8,128)(2,1)} %get-tuple-element.52), channel_id=1, source_target_pairs={{9,0},{10,1},{11,2},{12,3},{13,4},{14,5},{15,6},{17,8},{18,9},{19,... | collective-permute-start | bytes 49160 | tf_op jit(solution)/shard_map/ppermute | solution.py:31
  98.3 0.6 copy-start.20
  98.3 0.6 copy-start.8
  98.3 0.6 copy-start.9
  98.3 0.7 copy-start.4
  98.4 0.7 copy-start.5
  98.4 0.8 copy-start.1
where the time goes:
time: 128 us; the launch traced here: 126 us
  Pallas kernels  47.4 us (37%)
  starting transfers between devices  42.7 us (33%)
  waiting for transfers between devices  21.8 us (17%)
  blocking collectives  11.3 us (9%)
  local copies, waits for them, and re-layouts  1.42 us (1%)
    pallas_call x5, Pallas kernels, call(): pl.pallas_call(kernel, out_shape=outs, in_specs=[spec(index) for index in...  47.4 us
    ppermute x16, starting transfers between devices, shifted(): return lax.ppermute(value, ('ctx', 'tile'), pairs)  36.4 us
    ppermute x16, waiting for transfers between devices, shifted(): return lax.ppermute(value, ('ctx', 'tile'), pairs)  21.8 us
    all_to_all x1, blocking collectives, local(): pieces = lax.all_to_all(partial.reshape(tiles, -1, channels), 'tile', 0, 0)  11.3 us
    all_to_all x1, starting transfers between devices, local(): lax.all_to_all(embed.reshape(bands, band_tokens, -1), 'ctx', 0, 0)  3.67 us
    all_to_all x1, starting transfers between devices, local(): lax.all_to_all(chunks.reshape(bands * tiles, -1, channels), ('ctx', 'tile...  2.6 us
  transfers between devices with their start and end apart: 18, of which 3 were waited for; matrix products, arithmetic and copies ran while one was open for 0% of the time, Pallas kernels for 14%

commit v1 on v0

--- a/solution.py
+++ b/solution.py
@@ -20,29 +20,26 @@
 REGION_LANE, LOW_LANE, ONE_LANE = 2 * ROUNDS, 32, 64
 
 
-def shifted(value, down, right):
-    bands, tiles = lax.axis_size("ctx"), lax.axis_size("tile")
-    pairs = [
-        (i * tiles + j, (i + down) * tiles + j + right)
-        for i in range(bands)
-        for j in range(tiles)
-        if 0 <= i + down < bands and 0 <= j + right < tiles
-    ]
-    return lax.ppermute(value, ("ctx", "tile"), pairs)
-
-
-def exchange(sides):
-    top, bottom, first, last, top_first, top_last, bottom_first, bottom_last = sides
-    return (
-        shifted(bottom, 1, 0),
-        shifted(top, -1, 0),
-        shifted(last, 0, 1),
-        shifted(first, 0, -1),
-        shifted(bottom_last, 1, 1),
-        shifted(bottom_first, 1, -1),
-        shifted(top_last, -1, 1),
-        shifted(top_first, -1, -1),
-    )
+def shifted(value, axis, step):
+    size = lax.axis_size(axis)
+    pairs = [(i, i + step) for i in range(size) if 0 <= i + step < size]
+    return lax.ppermute(value, axis, pairs)
+
+
+def row_halo(top, bottom):
+    return shifted(bottom, "ctx", 1), shifted(top, "ctx", -1)
+
+
+def col_halo(cols, above, top, bottom, below):
+    rows = 4 * top.shape[0] // cols
+    first, last = call(
+        functools.partial(edges_kernel, cols),
+        "edges",
+        (above, top, bottom, below),
+        [array(rows * HALF, top.shape[1], BF16)] * 2,
+        grant=8,
+    )
+    return shifted(last, "tile", 1), shifted(first, "tile", -1)
 
 
 def matmul(left, right):
@@ -97,26 +94,24 @@
     return jax.ShapeDtypeStruct((count, lanes), dtype)
 
 
-def side_arrays(half, lanes):
-    edge = HALF * HALF
-    return [array(count, lanes, BF16) for count in (half, half, 2 * edge, 2 * edge, edge, edge, edge, edge)]
-
-
-def write_sides(sides, rows, cols):
-    top, bottom, first, last, *corners = sides
-    edges = []
-    for r, values in enumerate(rows):
-        half = (top, bottom)[r // HALF]
-        half[r % HALF * cols : (r % HALF + 1) * cols] = values.astype(BF16)
-    for begin in (0, cols - HALF):
-        edges.append(jnp.concatenate([values[begin : begin + HALF] for values in rows]).astype(BF16))
-    first[...], last[...] = edges
-    edge = HALF * HALF
-    for at, corner in enumerate(corners):
-        corner[...] = edges[at % 2][at // 2 * edge : (at // 2 + 1) * edge]
-
-
-def message_kernel(syndrome, region, state, *sides):
+def edges_kernel(cols, *refs):
+    parts, (first, last) = refs[:-2], refs[-2:]
+    firsts, lasts = [], []
+    for part in parts:
+        values = part[...].astype(F32)
+        for at in range(0, part.shape[0], cols):
+            firsts.append(values[at : at + HALF])
+            lasts.append(values[at + cols - HALF : at + cols])
+    first[...] = jnp.concatenate(firsts).astype(BF16)
+    last[...] = jnp.concatenate(lasts).astype(BF16)
+
+
+def write_halves(top, bottom, r, values):
+    half, count = (top, bottom)[r // HALF], values.shape[0]
+    half[r % HALF * count : (r % HALF + 1) * count] = values.astype(BF16)
+
+
+def message_kernel(syndrome, region, state, top, bottom):
     planes, rows, cols = syndrome.shape
     bits = syndrome[...].reshape(planes * rows, cols).astype(F32).astype(BF16)
     column_bits = matmul_nt(one_hot(iota((cols, cols), 0) == iota((cols, cols), 1)), bits).astype(BF16)
@@ -126,13 +121,12 @@
     column_region = matmul_nt(spread, regions.astype(BF16)).astype(BF16)
     plane, lane = iota((planes * rows, LANES), 0), iota((planes * rows, LANES), 1)
     ones = jnp.where((iota((cols, LANES), 1) == ONE_LANE) | (iota((cols, LANES), 1) == ONE_LANE + 1), 1.0, 0.0)
-    cells = []
     for r in range(rows):
         place = one_hot((plane == lane * rows + r) | (plane == (lane - LOW_LANE) * rows + r))
         region_place = one_hot((iota((8, LANES), 0) == r // 2) & (iota((8, LANES), 1) == REGION_LANE))
         flags = matmul(column_bits, place) + matmul(column_region, region_place) + ones
-        cells.append(jnp.concatenate([state[r * cols : (r + 1) * cols].astype(F32), flags], axis=1))
-    write_sides(sides, cells, cols)
+        cells = jnp.concatenate([state[r * cols : (r + 1) * cols], flags.astype(BF16)], axis=1)
+        write_halves(top, bottom, r, cells)
 
 
 def fetch(sources, targets, sems):
@@ -174,18 +168,15 @@
             self.state[j, at] = values[:, j * LANES : (j + 1) * LANES]
 
     def fill(self, parts, halo, put):
-        above, below, left, right, above_left, above_right, below_left, below_right = halo
+        above, below, left, right = halo
         parts = (above, *parts, below)
         r = 0
         for part in parts:
             for at in range(0, part.shape[0], self.cols):
                 put(pl.ds(r * self.span + self.width, self.cols), part[at : at + self.cols].astype(F32))
                 r += 1
-        for parts, first in (
-            ((above_left, left, below_left), 0),
-            ((above_right, right, below_right), self.width + self.cols),
-        ):
-            values = jnp.concatenate([part[...].astype(F32) for part in parts])
+        for part, first in ((left, 0), (right, self.width + self.cols)):
+            values = part[...].astype(F32)
             for r in range(self.rows):
                 put(pl.ds(r * self.span + first, self.width), values[r * self.width : (r + 1) * self.width])
 
@@ -197,18 +188,20 @@
             moved = values if b == 1 else pltpu.roll(values, 1 if b == 0 else size - 1, 0)
             self.taps[slot, first : first + size, b * self.channels : (b + 1) * self.channels] = moved.astype(BF16)
 
+    def begin(self):
+        part = self.count // 2
+        for first in range(0, self.count, part):
+            self.keep(0, first, self.get(pl.ds(first, part)))
+
     def advance(self, first_round, flags, conv, gate_weight, bit_weight):
         span, channels, rows = self.span, self.channels, self.rows
-        for first in range(0, rows, rows // 2):
-            self.keep(0, first * span, self.get(pl.ds(first * span, rows // 2 * span)))
         lane = iota((1, LANES), 1)
         for step in range(HALF):
             t, slot = first_round + step, step % 2
             now = (lane == 2 * t) | (lane == 2 * t + 1) | (lane == LOW_LANE + 2 * t) | (lane == LOW_LANE + 2 * t + 1)
             self.bits[...] = flags[...] * one_hot(now | (lane >= ONE_LANE))
             total = rows - 2 * (step + 1)
-            cut = (total // 4 + total // 2 % 2) * 2
-            for begin, part_rows in ((step + 1, cut), (step + 1 + cut, total - cut)):
+            for begin, part_rows in ((step + 1, total),):
                 first, size = begin * span, part_rows * span
                 columns = jnp.concatenate(
                     [self.taps[slot, first + a * span : first + a * span + size] for a in (-1, 0, 1)], axis=1
@@ -242,9 +235,9 @@
 
 
 def first_kernel(cols, top, bottom, *refs):
-    halo, (region, bit_weight, conv_hbm, gate_hbm) = refs[:8], refs[8:12]
-    (exact, partial, flags), sides = refs[12:15], refs[15:23]
-    state, taps, bits, mask, flags_wide, conv, gate_weight, sems = refs[23:]
+    halo, (region, bit_weight, conv_hbm, gate_hbm) = refs[:4], refs[4:8]
+    exact, partial, flags, new_top, new_bottom = refs[8:13]
+    state, taps, bits, mask, flags_wide, conv, gate_weight, sems = refs[13:]
     copies = fetch((conv_hbm, gate_hbm), (conv, gate_weight), sems)
     patch = Patch(cols, state, taps, bits, mask)
     channels = patch.channels
@@ -256,15 +249,16 @@
     patch.fill((top, bottom), halo, put)
     flags[...] = flags_wide[...].astype(BF16)
     mask[...] = mask_of(flags[...])
+    patch.begin()
     for copy in copies:
         copy.wait()
     patch.advance(0, flags, conv, gate_weight, bit_weight)
 
     own = patch.rows - 2 * patch.width
-    cells = [patch.own(r) for r in range(own)]
     for r in range(own):
-        exact[r * cols : (r + 1) * cols] = cells[r]
-    write_sides(sides, cells, cols)
+        values = patch.own(r)
+        exact[r * cols : (r + 1) * cols] = values
+        write_halves(new_top, new_bottom, r, values)
     block_cols = cols // 2
     total = jnp.zeros(partial.shape, F32)
     for r in range(0, own, 2):
@@ -290,8 +284,7 @@
 
 
 def second_kernel(
-    cols, bands, band_index, exact, above, below, left, right, above_left, above_right, below_left, below_right,
-    flags, sums, embed, attn_gain, mlp_gain, bit_weight,
+    cols, bands, band_index, exact, above, below, left, right, flags, sums, embed, attn_gain, mlp_gain, bit_weight,
     pool_hbm, key_hbm, value_hbm, query_hbm, out_hbm, up_hbm, down_hbm, return_hbm, conv_hbm, gate_hbm,
     state_out, context_out,
     state, taps, bits, mask, pool_weight, key_weight, value_weight, query_weight, out_weight, up_weight,
@@ -305,8 +298,7 @@
         sems,
     )
     patch = Patch(cols, state, taps, bits, mask)
-    halo = (above, below, left, right, above_left, above_right, below_left, below_right)
-    patch.fill((exact,), halo, patch.put)
+    patch.fill((exact,), (above, below, left, right), patch.put)
     mask[...] = mask_of(flags[...])
     region = matmul(flags[...], one_hot(iota((LANES, LANES), 0) == REGION_LANE))
     member[...] = jnp.where(region == iota(region.shape, 1).astype(F32), 1.0, 0.0)
@@ -377,6 +369,7 @@
 
     copies[8].wait()
     copies[9].wait()
+    patch.begin()
     patch.advance(HALF, flags, conv, gate_weight, bit_weight)
     for r in range(patch.rows - 2 * patch.width):
         state_out[r * cols : (r + 1) * cols] = patch.own(r).astype(BF16)
@@ -393,14 +386,14 @@
     conv = conv_weight.reshape(9 * channels, channels)
     half = HALF * cols
 
-    sides = call(
+    top, bottom = call(
         message_kernel,
         "message",
         (syndrome_bits.reshape(2 * ROUNDS, rows, cols), region_assign, state_in.reshape(rows * cols, channels)),
-        side_arrays(half, channels + LANES),
-    )
-    halo = exchange(sides)
-    embed, _ = lax.optimization_barrier((region_embed, sides[0]))
+        [array(half, channels + LANES, BF16)] * 2,
+    )
+    above, below = row_halo(top, bottom)
+    embed, _ = lax.optimization_barrier((region_embed, top))
     bit_weight, embed = call(
         prepare_kernel,
         "prepare",
@@ -408,29 +401,31 @@
         [array(LANES, 2 * channels, BF16), array(bands * band_tokens, embed_width, BF16)],
         moved=8 * MIB,
     )
-    embed, *rows_halo = lax.optimization_barrier((embed, *halo[:2]))
-    halo = (*rows_halo, *halo[2:])
+    embed, bit_weight, above, below = lax.optimization_barrier((embed, bit_weight, above, below))
+    left, right = col_halo(cols, above, top, bottom, below)
     embed = lax.all_to_all(embed.reshape(bands, band_tokens, -1), "ctx", 0, 0).reshape(-1, embed_width)
 
     count = (rows + 2 * HALF) * (cols + 2 * HALF)
     flops = 15 * rows * cols * HALF * 2 * channels * channels
-    exact, partial, flags, *new_sides = call(
+    exact, partial, flags, top, bottom = call(
         functools.partial(first_kernel, cols),
         "rounds",
-        (*sides[:2], *halo, region_assign, bit_weight, conv, gate_weight),
+        (top, bottom, above, below, left, right, region_assign, bit_weight, conv, gate_weight),
         [array(rows * cols, channels, F32), array(band_tokens, channels, BF16), array(count, LANES, BF16)]
-        + side_arrays(half, channels),
+        + [array(half, channels, BF16)] * 2,
         patch_scratch(rows, cols, channels)
         + [
             pltpu.VMEM((count, LANES), F32), pltpu.VMEM(conv.shape, BF16), pltpu.VMEM(gate_weight.shape, BF16),
             pltpu.SemaphoreType.DMA((2,)),
         ],
-        in_hbm=(12, 13),
+        in_hbm=(8, 9),
         flops=flops,
     )
 
     partial, embed = lax.optimization_barrier((partial, embed))
     pieces = lax.all_to_all(partial.reshape(tiles, -1, channels), "tile", 0, 0)
+    above, below = row_halo(top, bottom)
+    pieces, above, below = lax.optimization_barrier((pieces, above, below))
     (chunks,) = call(
         functools.partial(chunk_kernel, tiles),
         "chunk",
@@ -439,7 +434,8 @@
         grant=8,
     )
     sums = lax.all_to_all(chunks.reshape(bands * tiles, -1, channels), ("ctx", "tile"), 0, 0)
-    halo = exchange(new_sides)
+    above, below, _ = lax.optimization_barrier((above, below, chunks))
+    left, right = col_halo(cols, above, top, bottom, below)
 
     layer = (
         pool_weight, key_weight, value_weight, query_weight, out_weight, mlp_up, mlp_down, return_weight, conv,
@@ -452,8 +448,8 @@
         functools.partial(second_kernel, cols, bands),
         "context",
         (
-            lax.axis_index("ctx").reshape(1), exact, *halo, flags, sums.reshape(all_tokens, channels), embed,
-            attn_norm_gain[None], mlp_norm_gain[None], bit_weight, *layer,
+            lax.axis_index("ctx").reshape(1), exact, above, below, left, right, flags,
+            sums.reshape(all_tokens, channels), embed, attn_norm_gain[None], mlp_norm_gain[None], bit_weight, *layer,
         ),
         [array(rows * cols, channels, BF16), array(band_tokens, embed_width, BF16)],
         patch_scratch(rows, cols, channels)
@@ -466,7 +462,7 @@
             pltpu.VMEM((layer_rows, embed_width), BF16), pltpu.VMEM((layer_rows, mlp_up.shape[1]), BF16),
             pltpu.VMEM((layer_rows, embed_width), BF16), pltpu.SemaphoreType.DMA((len(layer),)),
         ],
-        in_hbm=range(16, 16 + len(layer)),
+        in_hbm=range(12, 12 + len(layer)),
         scalars=(0,),
         flops=2 * flops,
     )

time: 128 us -> 112 us (0.88); the launches traced: 126 us -> 111 us
  blocking collectives: 11.3 us -> 0 us
  starting transfers between devices: 42.7 us -> 33.8 us
  local copies, waits for them, and re-layouts: 1.42 us -> 5.1 us
  waiting for transfers between devices: 21.8 us -> 23.6 us
    ppermute x16 -> x8, starting transfers between devices: 36.4 us -> 17.5 us  [shifted(): return lax.ppermute(value, axis, pairs)]
    all_to_all x1 -> x0, blocking collectives: 11.3 us -> none  [local(): pieces = lax.all_to_all(partial.reshape(tiles, -1, channels), 'tile', 0, 0)]
    all_to_all x1, waiting for transfers between devices: 0.01 us -> 8.04 us  [local(): lax.all_to_all(chunks.reshape(bands * tiles, -1, channels), ('ctx', 'tile...]
    all_to_all x0 -> x1, starting transfers between devices: none -> 7.77 us  [local(): pieces = lax.all_to_all(partial.reshape(tiles, -1, channels), 'tile', 0, 0)]
    ppermute x16 -> x8, waiting for transfers between devices: 21.8 us -> 15.6 us  [shifted(): return lax.ppermute(value, axis, pairs)]
    unnamed x42 -> x28, local copies, waits for them, and re-layouts: 1.42 us -> 5.1 us
    all_to_all x1, starting transfers between devices: 2.6 us -> 5.02 us  [local(): lax.all_to_all(chunks.reshape(bands * tiles, -1, channels), ('ctx', 'tile...]
    pallas_call x5 -> x7, Pallas kernels: 47.4 us -> 47.5 us  [call(): pl.pallas_call(kernel, out_shape=outs, in_specs=[spec(index) for index in...]
  transfers between devices with their start and end apart: 18 -> 11, of which waited for: 3 -> 7; matrix products, arithmetic and copies ran while one was open for 0% -> 0% of each run, Pallas kernels for 14% -> 16%
where the time goes in v1:
time: 112 us; the launch traced here: 111 us
  Pallas kernels  47.5 us (42%)
  starting transfers between devices  33.8 us (30%)
  waiting for transfers between devices  23.6 us (21%)
  local copies, waits for them, and re-layouts  5.1 us (5%)
    pallas_call x7, Pallas kernels, call(): pl.pallas_call(kernel, out_shape=outs, in_specs=[spec(index) for index in...  47.5 us
    ppermute x8, starting transfers between devices, shifted(): return lax.ppermute(value, axis, pairs)  17.5 us
    ppermute x8, waiting for transfers between devices, shifted(): return lax.ppermute(value, axis, pairs)  15.6 us
    all_to_all x1, waiting for transfers between devices, local(): lax.all_to_all(chunks.reshape(bands * tiles, -1, channels), ('ctx', 'tile...  8.04 us
    all_to_all x1, starting transfers between devices, local(): pieces = lax.all_to_all(partial.reshape(tiles, -1, channels), 'tile', 0, 0)  7.77 us
    unnamed x28, local copies, waits for them, and re-layouts  5.1 us
    all_to_all x1, starting transfers between devices, local(): lax.all_to_all(chunks.reshape(bands * tiles, -1, channels), ('ctx', 'tile...  5.02 us
    all_to_all x1, starting transfers between devices, local(): lax.all_to_all(embed.reshape(bands, band_tokens, -1), 'ctx', 0, 0)  3.53 us
  transfers between devices with their start and end apart: 11, of which 7 were waited for; matrix products, arithmetic and copies ran while one was open for 0% of the time, Pallas kernels for 16%

profile of v1, /device:TPU:0, one launch (start us, length us, event | category | flops | bytes accessed | tf_op | source)
XLA Modules:
  0.0 111.0 jit_solution(8420979150265305450)
XLA Ops:
  0.6 2.0 %message.1 = (bf16[128,640]{1,0:T(8,128)(2,1)}, bf16[128,640]{1,0:T(8,128)(2,1)}) custom-call(s32[16,8,32]{2,1,0:T(8,128)} %bitcast.20, s32[4,16]{1,0:T(4,128)} %refs_4_.1, bf16[256,512]{1,0:T(8,128)(2,1)} %bitcast.18), custom_call_target="tpu_custom_call" | custom-call | bytes 1048576 | tf_op jit(solution)/shard_map/message/pallas_call | solution.py:81
  2.7 4.8 %collective-permute-start = (bf16[128,640]{1,0:T(8,128)(2,1)}, bf16[128,640]{1,0:T(8,128)(2,1)S(1)}, u32[]{:S(2)}, u32[]{:S(2)}) collective-permute-start(bf16[128,640]{1,0:T(8,128)(2,1)} %get-tuple-element.30.refs_2_.bottom), channel_id=1, source_target_pairs={{0,8},{8,16},{16,24},{1,9},{9,17},{17,25},{2,10},{10,18},{18,26},{... | collective-permute-start | bytes 491528 | tf_op jit(solution)/shard_map/ppermute | solution.py:26
  7.5 1.3 %collective-permute-start.1 = (bf16[128,640]{1,0:T(8,128)(2,1)}, bf16[128,640]{1,0:T(8,128)(2,1)S(1)}, u32[]{:S(2)}, u32[]{:S(2)}) collective-permute-start(bf16[128,640]{1,0:T(8,128)(2,1)} %get-tuple-element.29.refs_1_.top), channel_id=1, source_target_pairs={{8,0},{16,8},{24,16},{9,1},{17,9},{25,17},{10,2},{18,10},{26,18},{... | collective-permute-start | bytes 491528 | tf_op jit(solution)/shard_map/ppermute | solution.py:26
  8.8 2.2 %prepare.1 = (bf16[128,1024]{1,0:T(8,128)(2,1)}, bf16[512,1024]{1,0:T(8,128)(2,1)}) custom-call(f32[2,512]{1,0:T(2,128)} %candidate_bits.1, f32[2,512]{1,0:T(2,128)} %gate_bits.1, f32[1,512]{1,0:T(1,128)} %bitcast.21, bf16[128,1024]{1,0:T(8,128)(2,1)} %embed), custom_call_target="tpu_custom_call" | custom-call | bytes 8388608 | tf_op jit(solution)/shard_map/prepare/pallas_call | solution.py:81
  11.0 0.3 collective-permute-done.refs_0_
  11.3 0.0 copy-start.2
  11.3 5.3 %collective-permute-done.1.refs_3_.refs_1_ = bf16[128,640]{1,0:T(8,128)(2,1)S(1)} collective-permute-done((bf16[128,640]{1,0:T(8,128)(2,1)}, bf16[128,640]{1,0:T(8,128)(2,1)S(1)}, u32[]{:S(2)}, u32[]{:S(2)}) %collective-permute-start.1) | collective-permute-done | bytes 163872 | tf_op jit(solution)/shard_map/ppermute | solution.py:26
  16.6 0.0 copy-start.3
  16.6 0.0 copy-start
  16.6 1.0 copy-done
  17.6 0.0 copy-start.1
  17.6 0.9 copy-done.1
  18.5 0.1 edges.2
  18.6 1.3 %collective-permute-start.2 = (bf16[64,640]{1,0:T(8,128)(2,1)S(1)}, bf16[64,640]{1,0:T(8,128)(2,1)S(1)}, u32[]{:S(2)}, u32[]{:S(2)}) collective-permute-start(bf16[64,640]{1,0:T(8,128)(2,1)S(1)} %get-tuple-element.36), channel_id=1, source_target_pairs={{0,1},{1,2},{2,3},{3,4},{4,5},{5,6},{6,7},{8,9},{9,10},{10,11},{11... | collective-permute-start | bytes 245768 | tf_op jit(solution)/shard_map/ppermute | solution.py:26
  19.9 1.3 %collective-permute-start.3 = (bf16[64,640]{1,0:T(8,128)(2,1)S(1)}, bf16[64,640]{1,0:T(8,128)(2,1)S(1)}, u32[]{:S(2)}, u32[]{:S(2)}) collective-permute-start(bf16[64,640]{1,0:T(8,128)(2,1)S(1)} %get-tuple-element.37), channel_id=1, source_target_pairs={{1,0},{2,1},{3,2},{4,3},{5,4},{6,5},{7,6},{9,8},{10,9},{11,10},{12... | collective-permute-start | bytes 245768 | tf_op jit(solution)/shard_map/ppermute | solution.py:26
  21.2 3.5 %all-to-all-start = ((bf16[4,128,1024]{2,1,0:T(8,128)(2,1)}), bf16[4,128,1024]{2,1,0:T(8,128)(2,1)S(1)}, u32[]{:S(2)}, u32[]{:S(2)}) async-start(bf16[4,128,1024]{2,1,0:T(8,128)(2,1)} %bitcast.16), calls=%async_computation | async-start | bytes 2097152 | tf_op jit(solution)/shard_map/all_to_all | solution.py:406
  24.7 0.0 collective-permute-done.2.refs_2_
  24.7 0.0 copy-start.10
  24.7 0.1 collective-permute-done.3.refs_3_
  24.9 0.0 copy-start.11
  24.9 0.0 copy-done.2
  24.9 0.0 copy-done.3
  24.9 0.5 copy-done.10
  25.4 0.1 copy-done.11
  25.5 15.8 %rounds.1 = (f32[256,512]{1,0:T(8,128)}, bf16[128,512]{1,0:T(8,128)(2,1)}, bf16[640,128]{1,0:T(8,128)(2,1)}, bf16[128,512]{1,0:T(8,128)(2,1)}, bf16[128,512]{1,0:T(8,128)(2,1)}) custom-call(bf16[128,640]{1,0:T(8,128)(2,1)} %get-tuple-element.29.refs_1_.top, bf16[128,640]{1,0:T(8,128)(2,1)} %get-tuple-element.30.refs_2_.bottom, bf16[128,640]{1,0:T(8,128)(2,1)} %copy-done.2, ...), custom_call_target="tpu_custom_call" | custom-call | flops 8053063680 | bytes 1048576 | tf_op jit(solution)/shard_map/rounds/pallas_call | solution.py:81
  41.2 0.0 all-to-all-done
  41.2 0.0 copy-start.8
  41.3 7.8 %all-to-all-start.1 = ((bf16[8,16,512]{2,1,0:T(8,128)(2,1)}), bf16[8,16,512]{2,1,0:T(8,128)(2,1)S(1)}, u32[]{:S(2)}, u32[]{:S(2)}) async-start(bf16[8,16,512]{2,1,0:T(8,128)(2,1)} %bitcast.19), calls=%async_computation.1 | async-start | bytes 262144 | tf_op jit(solution)/shard_map/all_to_all | solution.py:426
  49.0 3.9 %collective-permute-start.4 = (bf16[128,512]{1,0:T(8,128)(2,1)}, bf16[128,512]{1,0:T(8,128)(2,1)S(1)}, u32[]{:S(2)}, u32[]{:S(2)}) collective-permute-start(bf16[128,512]{1,0:T(8,128)(2,1)} %get-tuple-element.43.refs_2_), channel_id=1, source_target_pairs={{0,8},{8,16},{16,24},{1,9},{9,17},{17,25},{2,10},{10,18},{18,26},{... | collective-permute-start | bytes 393224 | tf_op jit(solution)/shard_map/ppermute | solution.py:26
  52.9 1.3 %collective-permute-start.5 = (bf16[128,512]{1,0:T(8,128)(2,1)}, bf16[128,512]{1,0:T(8,128)(2,1)S(1)}, u32[]{:S(2)}, u32[]{:S(2)}) collective-permute-start(bf16[128,512]{1,0:T(8,128)(2,1)} %get-tuple-element.44.refs_1_), channel_id=1, source_target_pairs={{8,0},{16,8},{24,16},{9,1},{17,9},{25,17},{10,2},{18,10},{26,18},{... | collective-permute-start | bytes 393224 | tf_op jit(solution)/shard_map/ppermute | solution.py:26
  54.2 2.4 %collective-permute-done.4.refs_0_.above = bf16[128,512]{1,0:T(8,128)(2,1)S(1)} collective-permute-done((bf16[128,512]{1,0:T(8,128)(2,1)}, bf16[128,512]{1,0:T(8,128)(2,1)S(1)}, u32[]{:S(2)}, u32[]{:S(2)}) %collective-permute-start.4) | collective-permute-done | bytes 131104 | tf_op jit(solution)/shard_map/ppermute | solution.py:26
  56.6 0.0 copy-start.4
  56.6 4.6 %collective-permute-done.5.refs_3_.below = bf16[128,512]{1,0:T(8,128)(2,1)S(1)} collective-permute-done((bf16[128,512]{1,0:T(8,128)(2,1)}, bf16[128,512]{1,0:T(8,128)(2,1)S(1)}, u32[]{:S(2)}, u32[]{:S(2)}) %collective-permute-start.5) | collective-permute-done | bytes 131104 | tf_op jit(solution)/shard_map/ppermute | solution.py:26
  61.3 0.0 copy-start.5
  61.3 0.0 all-to-all-done.1
  61.3 0.9 chunk.1
  62.1 5.0 %all-to-all-start.2 = ((bf16[32,16,512]{2,1,0:T(8,128)(2,1)}), bf16[32,16,512]{2,1,0:T(8,128)(2,1)S(1)}, u32[]{:S(2)}, u32[]{:S(2)}) async-start(bf16[32,16,512]{2,1,0:T(8,128)(2,1)} %bitcast.9), calls=%async_computation.2 | async-start | bytes 1048576 | tf_op jit(solution)/shard_map/all_to_all | solution.py:436
  67.1 0.0 copy-start.6
  67.2 0.9 copy-done.6
  68.1 0.0 copy-start.7
  68.1 0.9 copy-done.7
  69.0 2.2 %collective-permute-start.6 = (bf16[64,512]{1,0:T(8,128)(2,1)S(1)}, bf16[64,512]{1,0:T(8,128)(2,1)S(1)}, u32[]{:S(2)}, u32[]{:S(2)}) collective-permute-start(bf16[64,512]{1,0:T(8,128)(2,1)S(1)} %get-tuple-element.50), channel_id=1, source_target_pairs={{0,1},{1,2},{2,3},{3,4},{4,5},{5,6},{6,7},{8,9},{9,10},{10,11},{11... | collective-permute-start | bytes 196616 | tf_op jit(solution)/shard_map/ppermute | solution.py:26
  71.2 1.5 %collective-permute-start.7 = (bf16[64,512]{1,0:T(8,128)(2,1)S(1)}, bf16[64,512]{1,0:T(8,128)(2,1)S(1)}, u32[]{:S(2)}, u32[]{:S(2)}) collective-permute-start(bf16[64,512]{1,0:T(8,128)(2,1)S(1)} %get-tuple-element.51), channel_id=1, source_target_pairs={{1,0},{2,1},{3,2},{4,3},{5,4},{6,5},{7,6},{9,8},{10,9},{11,10},{12... | collective-permute-start | bytes 196616 | tf_op jit(solution)/shard_map/ppermute | solution.py:26
  72.7 0.0 collective-permute-done.6.left
  72.7 0.0 copy-start.12
  72.7 2.8 %collective-permute-done.7.right = bf16[64,512]{1,0:T(8,128)(2,1)S(1)} collective-permute-done((bf16[64,512]{1,0:T(8,128)(2,1)S(1)}, bf16[64,512]{1,0:T(8,128)(2,1)S(1)}, u32[]{:S(2)}, u32[]{:S(2)}) %collective-permute-start.7) | collective-permute-done | bytes 65568 | tf_op jit(solution)/shard_map/ppermute | solution.py:26
  75.5 0.0 copy-start.13
  75.5 8.0 %all-to-all-done.2 = bf16[32,16,512]{2,1,0:T(8,128)(2,1)S(1)} async-done(((bf16[32,16,512]{2,1,0:T(8,128)(2,1)}), bf16[32,16,512]{2,1,0:T(8,128)(2,1)S(1)}, u32[]{:S(2)}, u32[]{:S(2)}) %all-to-all-start.2) | async-done | bytes 524320 | tf_op jit(solution)/shard_map/all_to_all | solution.py:436
  83.5 0.0 copy-start.9
  83.5 0.0 copy-done.8
  83.5 0.0 copy-done.4
  83.5 0.0 copy-done.5
  83.5 0.0 copy-done.12
  83.5 0.0 copy-done.13
  83.5 0.8 copy-done.9
  84.3 26.6 %context.1 = (bf16[256,512]{1,0:T(8,128)(2,1)}, bf16[128,1024]{1,0:T(8,128)(2,1)}) custom-call(s32[1]{0:T(128)} %bitcast.band_index, f32[256,512]{1,0:T(8,128)} %get-tuple-element.39.exact, bf16[128,512]{1,0:T(8,128)(2,1)} %copy-done.4, bf16[128,512]{1,0:T(8,128)(2,1)} %copy-done.5, bf16[64,512]{1,0:T(8,128)(2,1)} %copy-done.12, bf16[64,512]{1,0:T(8,128)(2,1)} %copy-done.13, ...), custom_call_target="tpu_custom_call" | custom-call | flops 16106127360 | bytes 1048576 | tf_op jit(solution)/shard_map/context/pallas_call | solution.py:81
  (1 shorter events, 0.0 us)
Async XLA Ops:
  2.7 8.6 %collective-permute-start = (bf16[128,640]{1,0:T(8,128)(2,1)}, bf16[128,640]{1,0:T(8,128)(2,1)S(1)}, u32[]{:S(2)}, u32[]{:S(2)}) collective-permute-start(bf16[128,640]{1,0:T(8,128)(2,1)} %get-tuple-element.30.refs_2_.bottom), channel_id=1, source_target_pairs={{0,8},{8,16},{16,24},{1,9},{9,17},{17,25},{2,10},{10,18},{18,26},{... | collective-permute-start | bytes 491528 | tf_op jit(solution)/shard_map/ppermute | solution.py:26
  7.5 9.1 %collective-permute-start.1 = (bf16[128,640]{1,0:T(8,128)(2,1)}, bf16[128,640]{1,0:T(8,128)(2,1)S(1)}, u32[]{:S(2)}, u32[]{:S(2)}) collective-permute-start(bf16[128,640]{1,0:T(8,128)(2,1)} %get-tuple-element.29.refs_1_.top), channel_id=1, source_target_pairs={{8,0},{16,8},{24,16},{9,1},{17,9},{25,17},{10,2},{18,10},{26,18},{... | collective-permute-start | bytes 491528 | tf_op jit(solution)/shard_map/ppermute | solution.py:26
  11.3 13.6 %copy-start.2 = (bf16[128,640]{1,0:T(8,128)(2,1)}, bf16[128,640]{1,0:T(8,128)(2,1)S(1)}, u32[]{:S(2)}) copy-start(bf16[128,640]{1,0:T(8,128)(2,1)S(1)} %collective-permute-done.refs_0_) | copy-start | bytes 491524
  16.6 8.2 %copy-start.3 = (bf16[128,640]{1,0:T(8,128)(2,1)}, bf16[128,640]{1,0:T(8,128)(2,1)S(1)}, u32[]{:S(2)}) copy-start(bf16[128,640]{1,0:T(8,128)(2,1)S(1)} %collective-permute-done.1.refs_3_.refs_1_) | copy-start | bytes 491524
  16.6 1.0 copy-start
  17.6 0.9 copy-start.1
  18.6 6.1 %collective-permute-start.2 = (bf16[64,640]{1,0:T(8,128)(2,1)S(1)}, bf16[64,640]{1,0:T(8,128)(2,1)S(1)}, u32[]{:S(2)}, u32[]{:S(2)}) collective-permute-start(bf16[64,640]{1,0:T(8,128)(2,1)S(1)} %get-tuple-element.36), channel_id=1, source_target_pairs={{0,1},{1,2},{2,3},{3,4},{4,5},{5,6},{6,7},{8,9},{9,10},{10,11},{11... | collective-permute-start | bytes 245768 | tf_op jit(solution)/shard_map/ppermute | solution.py:26
  19.9 5.0 %collective-permute-start.3 = (bf16[64,640]{1,0:T(8,128)(2,1)S(1)}, bf16[64,640]{1,0:T(8,128)(2,1)S(1)}, u32[]{:S(2)}, u32[]{:S(2)}) collective-permute-start(bf16[64,640]{1,0:T(8,128)(2,1)S(1)} %get-tuple-element.37), channel_id=1, source_target_pairs={{1,0},{2,1},{3,2},{4,3},{5,4},{6,5},{7,6},{9,8},{10,9},{11,10},{12... | collective-permute-start | bytes 245768 | tf_op jit(solution)/shard_map/ppermute | solution.py:26
  21.2 20.1 %all-to-all-start = ((bf16[4,128,1024]{2,1,0:T(8,128)(2,1)}), bf16[4,128,1024]{2,1,0:T(8,128)(2,1)S(1)}, u32[]{:S(2)}, u32[]{:S(2)}) async-start(bf16[4,128,1024]{2,1,0:T(8,128)(2,1)} %bitcast.16), calls=%async_computation | async-start | bytes 2097152 | tf_op jit(solution)/shard_map/all_to_all | solution.py:406
  24.7 0.6 copy-start.10
  24.9 0.6 copy-start.11
  41.2 42.3 %copy-start.8 = (bf16[4,128,1024]{2,1,0:T(8,128)(2,1)}, bf16[4,128,1024]{2,1,0:T(8,128)(2,1)S(1)}, u32[]{:S(2)}) copy-start(bf16[4,128,1024]{2,1,0:T(8,128)(2,1)S(1)} %all-to-all-done) | copy-start | bytes 3145732
  41.3 20.0 %all-to-all-start.1 = ((bf16[8,16,512]{2,1,0:T(8,128)(2,1)}), bf16[8,16,512]{2,1,0:T(8,128)(2,1)S(1)}, u32[]{:S(2)}, u32[]{:S(2)}) async-start(bf16[8,16,512]{2,1,0:T(8,128)(2,1)} %bitcast.19), calls=%async_computation.1 | async-start | bytes 262144 | tf_op jit(solution)/shard_map/all_to_all | solution.py:426
  49.0 7.6 %collective-permute-start.4 = (bf16[128,512]{1,0:T(8,128)(2,1)}, bf16[128,512]{1,0:T(8,128)(2,1)S(1)}, u32[]{:S(2)}, u32[]{:S(2)}) collective-permute-start(bf16[128,512]{1,0:T(8,128)(2,1)} %get-tuple-element.43.refs_2_), channel_id=1, source_target_pairs={{0,8},{8,16},{16,24},{1,9},{9,17},{17,25},{2,10},{10,18},{18,26},{... | collective-permute-start | bytes 393224 | tf_op jit(solution)/shard_map/ppermute | solution.py:26
  52.9 8.3 %collective-permute-start.5 = (bf16[128,512]{1,0:T(8,128)(2,1)}, bf16[128,512]{1,0:T(8,128)(2,1)S(1)}, u32[]{:S(2)}, u32[]{:S(2)}) collective-permute-start(bf16[128,512]{1,0:T(8,128)(2,1)} %get-tuple-element.44.refs_1_), channel_id=1, source_target_pairs={{8,0},{16,8},{24,16},{9,1},{17,9},{25,17},{10,2},{18,10},{26,18},{... | collective-permute-start | bytes 393224 | tf_op jit(solution)/shard_map/ppermute | solution.py:26
  56.6 26.9 %copy-start.4 = (bf16[128,512]{1,0:T(8,128)(2,1)}, bf16[128,512]{1,0:T(8,128)(2,1)S(1)}, u32[]{:S(2)}) copy-start(bf16[128,512]{1,0:T(8,128)(2,1)S(1)} %collective-permute-done.4.refs_0_.above) | copy-start | bytes 393220
  61.3 22.3 %copy-start.5 = (bf16[128,512]{1,0:T(8,128)(2,1)}, bf16[128,512]{1,0:T(8,128)(2,1)S(1)}, u32[]{:S(2)}) copy-start(bf16[128,512]{1,0:T(8,128)(2,1)S(1)} %collective-permute-done.5.refs_3_.below) | copy-start | bytes 393220
  62.1 21.4 %all-to-all-start.2 = ((bf16[32,16,512]{2,1,0:T(8,128)(2,1)}), bf16[32,16,512]{2,1,0:T(8,128)(2,1)S(1)}, u32[]{:S(2)}, u32[]{:S(2)}) async-start(bf16[32,16,512]{2,1,0:T(8,128)(2,1)} %bitcast.9), calls=%async_computation.2 | async-start | bytes 1048576 | tf_op jit(solution)/shard_map/all_to_all | solution.py:436
  67.1 0.9 copy-start.6
  68.1 0.9 copy-start.7
  69.0 3.7 %collective-permute-start.6 = (bf16[64,512]{1,0:T(8,128)(2,1)S(1)}, bf16[64,512]{1,0:T(8,128)(2,1)S(1)}, u32[]{:S(2)}, u32[]{:S(2)}) collective-permute-start(bf16[64,512]{1,0:T(8,128)(2,1)S(1)} %get-tuple-element.50), channel_id=1, source_target_pairs={{0,1},{1,2},{2,3},{3,4},{4,5},{5,6},{6,7},{8,9},{9,10},{10,11},{11... | collective-permute-start | bytes 196616 | tf_op jit(solution)/shard_map/ppermute | solution.py:26
  71.2 4.3 %collective-permute-start.7 = (bf16[64,512]{1,0:T(8,128)(2,1)S(1)}, bf16[64,512]{1,0:T(8,128)(2,1)S(1)}, u32[]{:S(2)}, u32[]{:S(2)}) collective-permute-start(bf16[64,512]{1,0:T(8,128)(2,1)S(1)} %get-tuple-element.51), channel_id=1, source_target_pairs={{1,0},{2,1},{3,2},{4,3},{5,4},{6,5},{7,6},{9,8},{10,9},{11,10},{12... | collective-permute-start | bytes 196616 | tf_op jit(solution)/shard_map/ppermute | solution.py:26
  72.7 10.9 %copy-start.12 = (bf16[64,512]{1,0:T(8,128)(2,1)}, bf16[64,512]{1,0:T(8,128)(2,1)S(1)}, u32[]{:S(2)}) copy-start(bf16[64,512]{1,0:T(8,128)(2,1)S(1)} %collective-permute-done.6.left) | copy-start | bytes 196612
  75.5 8.1 %copy-start.13 = (bf16[64,512]{1,0:T(8,128)(2,1)}, bf16[64,512]{1,0:T(8,128)(2,1)S(1)}, u32[]{:S(2)}) copy-start(bf16[64,512]{1,0:T(8,128)(2,1)S(1)} %collective-permute-done.7.right) | copy-start | bytes 196612
  83.5 0.8 copy-start.9
